TPU v7x, 32 devices: a whole 2x2x4 slice. The times are simulated.
32 devices in a mesh: groups: 2 (over y), seq: 8 (over z, x), head: 2 (over core).
Axes of the slice: x: 2, y: 2, z: 4, core: 2. Of those that a mesh axis runs over, the one named last changes fastest.
Arguments:
- tokens: bfloat16 [8192, 1024], P(('groups', 'seq')), parts along dimension 0, may hold values from -24 to 24
- w_qkv: bfloat16 [3, 1024, 512], P(None, None, 'head'), may hold values from -0.1875 to 0.1875
- w_out: bfloat16 [512, 1024], P('head'), may hold values from -0.25 to 0.25
- random_blocks: int32 [128, 3], P(('groups', 'seq')), parts along dimension 0, may hold values from 0 to 63, as said below
- global_ids: int32 [32], P('groups'), parts along dimension 0, may hold values from 0 to 63, as said below
Outputs:
- mixed: bfloat16 [8192, 1024], P(('groups', 'seq'), 'head'), parts along dimension 0
There are 2 independent parts, one for each index of `groups`. A program takes and returns all parts, laid end to end along the dimension named above; an argument that names none is the same for every part. Nothing has to cross between parts.
Inputs may be any that keep to these rules, and one draw needn't show every extreme that they name: `random_blocks`: each entry of row b is a block of the document; its index of seq, entry // 8, lies within 1 places of b // 8 around the closed cycle of seq, and some entry of every draw lies exactly 1 places ahead and another exactly 1 places behind. `global_ids`: distinct block numbers.
All inputs are finite; a program needn't handle non-finite values.
Results may differ from a plain program's by a relative error of at most 0.011.
Values may be sent and summed in bfloat16 or wider, within the bound.
A program may use at most 64 MiB of HBM per device.

v0:
```python
import math

import jax
import jax.numpy as jnp
from jax import lax
from jax.sharding import PartitionSpec as P

HEAD_DIM = 64
BLOCK = 64
RAND = 3


def padded_2(block, sides, width):
    for axis, dim in sides:
        count = lax.axis_size(axis)
        forward = [(i, i + 1) for i in range(count - 1)]
        forward.append((count - 1, 0))
        backward = [(target, source) for source, target in forward]
        low = lax.ppermute(
            lax.slice_in_dim(block, block.shape[dim] - width, None, axis=dim), axis, forward
        )
        high = lax.ppermute(lax.slice_in_dim(block, 0, width, axis=dim), axis, backward)
        block = jnp.concatenate([low, block, high], axis=dim)
    return block


def passed_along(block, axis, distance):
    devices = range(lax.axis_size(axis))
    route = [((i - distance) % len(devices), i) for i in devices]
    return lax.ppermute(block, axis, route)


def broadcast(shard, axis, root):
    mine = lax.axis_index(axis) == root
    return lax.psum(jnp.where(mine, shard, jnp.zeros_like(shard)), axis)


def attend_head(packed):
    single_query_head, local_block_pair, global_block_pair = packed
    scale_factor = 1.0 / math.sqrt(single_query_head.shape[-1])
    local_scores = (
        jnp.einsum(
            "vhw,vcw->vhc",
            single_query_head,
            local_block_pair[0],
            preferred_element_type=jnp.float32,
        )
        * scale_factor
    )
    global_scores = (
        jnp.einsum(
            "ors,is->ori",
            single_query_head,
            global_block_pair[0],
            preferred_element_type=jnp.float32,
        )
        * scale_factor
    )
    largest = jnp.maximum(
        jnp.max(local_scores, axis=-1, keepdims=True),
        jnp.max(global_scores, axis=-1, keepdims=True),
    )
    local_exp = jnp.exp(local_scores - largest)
    global_exp = jnp.exp(global_scores - largest)
    totals = jnp.sum(local_exp, axis=-1, keepdims=True) + jnp.sum(
        global_exp, axis=-1, keepdims=True
    )
    local_attention_weights = (local_exp / totals).astype(jnp.bfloat16)
    global_attention_weights = (global_exp / totals).astype(jnp.bfloat16)
    blended = jnp.einsum(
        "onw,owz->onz",
        local_attention_weights,
        local_block_pair[1],
        preferred_element_type=jnp.float32,
    )
    blended = blended + jnp.einsum(
        "sou,ug->sog",
        global_attention_weights,
        global_block_pair[1],
        preferred_element_type=jnp.float32,
    )
    return blended.astype(jnp.bfloat16)


def on_device(tokens, w_qkv, w_out, random_blocks, global_ids):
    cycle_size = lax.axis_size("seq")
    my_index = lax.axis_index("seq")
    reach_count = max(1, cycle_size // 64)
    tok_rows = tokens.shape[0]
    blk_count = tok_rows // BLOCK
    features = w_qkv.shape[2]
    head_count = features // HEAD_DIM
    queries = jnp.dot(tokens, w_qkv[0], preferred_element_type=jnp.float32).astype(jnp.bfloat16)
    key_rows = jnp.dot(tokens, w_qkv[1], preferred_element_type=jnp.float32).astype(jnp.bfloat16)
    value_rows = jnp.dot(tokens, w_qkv[2], preferred_element_type=jnp.float32).astype(jnp.bfloat16)
    paired_blocks = jnp.stack([key_rows, value_rows])
    pair_blocks = paired_blocks.reshape(2, blk_count, BLOCK, features)
    padded = padded_2(paired_blocks, (("seq", 1),), BLOCK)
    padded_blocks = padded.reshape(2, blk_count + 2, BLOCK, features)
    window = jnp.concatenate(
        [
            padded_blocks[:, 0:blk_count],
            padded_blocks[:, 1 : blk_count + 1],
            padded_blocks[:, 2 : blk_count + 2],
        ],
        axis=2,
    )
    flat_lists = random_blocks.reshape(-1)
    list_owner = flat_lists // blk_count
    list_within = flat_lists % blk_count
    relative = (list_owner - my_index) % cycle_size

    def pick_blocks(collected, piece, offset):
        taken = jnp.take(piece, list_within, axis=1)
        matches = relative == offset % cycle_size
        return jnp.where(matches[None, :, None, None], taken, collected)

    collected = jnp.zeros((2, blk_count * RAND, BLOCK, features), jnp.bfloat16)
    current = passed_along(pair_blocks, "seq", -reach_count)
    collected = pick_blocks(collected, current, reach_count)

    def advance(turn_index, carried):
        moving, gathered = carried
        moving = passed_along(moving, "seq", 1)
        return (moving, pick_blocks(gathered, moving, reach_count - turn_index))

    current, collected = lax.fori_loop(1, 2 * reach_count + 1, advance, (current, collected))
    global_owner = global_ids // blk_count
    global_within = global_ids % blk_count
    global_count = global_ids.shape[0]

    def fetch_global(slot_index, gathered):
        local_piece = lax.dynamic_index_in_dim(
            pair_blocks, global_within[slot_index], axis=1, keepdims=False
        )
        arrived = broadcast(local_piece, "seq", global_owner[slot_index])
        return lax.dynamic_update_index_in_dim(gathered, arrived, slot_index, axis=1)

    global_block_pair = lax.fori_loop(
        0, global_count, fetch_global, jnp.zeros((2, global_count, BLOCK, features), jnp.bfloat16)
    )
    local_block_pair = jnp.concatenate(
        [window, collected.reshape(2, blk_count, RAND * BLOCK, features)], axis=2
    )
    local_heads = local_block_pair.reshape(2, blk_count, -1, head_count, HEAD_DIM).transpose(
        3, 0, 1, 2, 4
    )
    global_heads = global_block_pair.reshape(
        2, global_count * BLOCK, head_count, HEAD_DIM
    ).transpose(2, 0, 1, 3)
    query_heads = queries.reshape(blk_count, BLOCK, head_count, HEAD_DIM).transpose(2, 0, 1, 3)
    attended = lax.map(attend_head, (query_heads, local_heads, global_heads))
    attention = attended.transpose(1, 2, 0, 3).reshape(tok_rows, features)
    partial_sum = jnp.dot(attention, w_out, preferred_element_type=jnp.float32)
    return lax.psum_scatter(
        partial_sum.astype(jnp.bfloat16), "head", scatter_dimension=1, tiled=True
    )


def solution(mesh):
    return jax.shard_map(
        on_device,
        mesh=mesh,
        in_specs=(
            P(("groups", "seq"), None),
            P(None, None, "head"),
            P("head", None),
            P(("groups", "seq"), None),
            P("groups"),
        ),
        out_specs=P(("groups", "seq"), "head"),
        check_vma=False,
    )
```

profile of v0, /device:TPU:1, one launch (start us, length us, event | category | flops | bytes accessed | tf_op | source)
XLA Modules:
  0.0 1367.5 jit_solution(11386260603527474855)
XLA Ops:
  11.4 5.1 collective-permute-start.3
  17.2 4.2 collective-permute-start.2
  23.2 1199.0 %while.41 = (s32[]{:T(128)}, bf16[2,16,64,256]{3,2,1,0:T(8,128)(2,1)}, s32[16]{0:T(128)S(1)}, s32[16]{0:T(128)S(1)}, bf16[2,8,64,256]{3,2,1,0:T(8,128)(2,1)}, /*...) while((s32[]{:T(128)}, bf16[2,16,64,256]{3,2,1,0:T(8,128)(2,1)}, s32[16]{0:T(128)S(1)}, ...), condition=%wide.region_4.6_spmd, body=%wide.region_2.5_spmd.sunk | while | flops 65545 | bytes 655617 | solution.py:139
  26.9 1.5 dynamic-slice_select_fusion.2
  28.4 64.9 %all-reduce.2.cloned.1.call-done = bf16[2,1,64,256]{3,2,1,0:T(8,128)(2,1)} async-done(((bf16[2,1,64,256]{3,2,1,0:T(8,128)(2,1)}), bf16[2,1,64,256]{3,2,1,0:T(8,128)(2,1)}) %all-reduce.2.cloned.1.call-update) | async-done | bytes 65552 | tf_op jit(solution)/shard_map/while/body/eval_jaxpr/psum | solution.py:35
  98.4 1.5 dynamic-slice_select_fusion.2
  99.9 68.6 %all-reduce.2.cloned.1.call-done = bf16[2,1,64,256]{3,2,1,0:T(8,128)(2,1)} async-done(((bf16[2,1,64,256]{3,2,1,0:T(8,128)(2,1)}), bf16[2,1,64,256]{3,2,1,0:T(8,128)(2,1)}) %all-reduce.2.cloned.1.call-update) | async-done | bytes 65552 | tf_op jit(solution)/shard_map/while/body/eval_jaxpr/psum | solution.py:35
  175.1 68.6 %all-reduce.2.cloned.1.call-done = bf16[2,1,64,256]{3,2,1,0:T(8,128)(2,1)} async-done(((bf16[2,1,64,256]{3,2,1,0:T(8,128)(2,1)}), bf16[2,1,64,256]{3,2,1,0:T(8,128)(2,1)}) %all-reduce.2.cloned.1.call-update) | async-done | bytes 65552 | tf_op jit(solution)/shard_map/while/body/eval_jaxpr/psum | solution.py:35
  248.8 1.5 dynamic-slice_select_fusion.2
  250.3 68.6 %all-reduce.2.cloned.1.call-done = bf16[2,1,64,256]{3,2,1,0:T(8,128)(2,1)} async-done(((bf16[2,1,64,256]{3,2,1,0:T(8,128)(2,1)}), bf16[2,1,64,256]{3,2,1,0:T(8,128)(2,1)}) %all-reduce.2.cloned.1.call-update) | async-done | bytes 65552 | tf_op jit(solution)/shard_map/while/body/eval_jaxpr/psum | solution.py:35
  325.4 68.6 %all-reduce.2.cloned.1.call-done = bf16[2,1,64,256]{3,2,1,0:T(8,128)(2,1)} async-done(((bf16[2,1,64,256]{3,2,1,0:T(8,128)(2,1)}), bf16[2,1,64,256]{3,2,1,0:T(8,128)(2,1)}) %all-reduce.2.cloned.1.call-update) | async-done | bytes 65552 | tf_op jit(solution)/shard_map/while/body/eval_jaxpr/psum | solution.py:35
  399.1 1.5 dynamic-slice_select_fusion.2
  400.6 68.6 %all-reduce.2.cloned.1.call-done = bf16[2,1,64,256]{3,2,1,0:T(8,128)(2,1)} async-done(((bf16[2,1,64,256]{3,2,1,0:T(8,128)(2,1)}), bf16[2,1,64,256]{3,2,1,0:T(8,128)(2,1)}) %all-reduce.2.cloned.1.call-update) | async-done | bytes 65552 | tf_op jit(solution)/shard_map/while/body/eval_jaxpr/psum | solution.py:35
  474.2 1.5 dynamic-slice_select_fusion.2
  475.7 68.6 %all-reduce.2.cloned.1.call-done = bf16[2,1,64,256]{3,2,1,0:T(8,128)(2,1)} async-done(((bf16[2,1,64,256]{3,2,1,0:T(8,128)(2,1)}), bf16[2,1,64,256]{3,2,1,0:T(8,128)(2,1)}) %all-reduce.2.cloned.1.call-update) | async-done | bytes 65552 | tf_op jit(solution)/shard_map/while/body/eval_jaxpr/psum | solution.py:35
  550.9 68.6 %all-reduce.2.cloned.1.call-done = bf16[2,1,64,256]{3,2,1,0:T(8,128)(2,1)} async-done(((bf16[2,1,64,256]{3,2,1,0:T(8,128)(2,1)}), bf16[2,1,64,256]{3,2,1,0:T(8,128)(2,1)}) %all-reduce.2.cloned.1.call-update) | async-done | bytes 65552 | tf_op jit(solution)/shard_map/while/body/eval_jaxpr/psum | solution.py:35
  626.0 68.6 %all-reduce.2.cloned.1.call-done = bf16[2,1,64,256]{3,2,1,0:T(8,128)(2,1)} async-done(((bf16[2,1,64,256]{3,2,1,0:T(8,128)(2,1)}), bf16[2,1,64,256]{3,2,1,0:T(8,128)(2,1)}) %all-reduce.2.cloned.1.call-update) | async-done | bytes 65552 | tf_op jit(solution)/shard_map/while/body/eval_jaxpr/psum | solution.py:35
  694.6 1.5 constant_dynamic-update-slice_fusion.2
  701.2 68.6 %all-reduce.2.cloned.1.call-done = bf16[2,1,64,256]{3,2,1,0:T(8,128)(2,1)} async-done(((bf16[2,1,64,256]{3,2,1,0:T(8,128)(2,1)}), bf16[2,1,64,256]{3,2,1,0:T(8,128)(2,1)}) %all-reduce.2.cloned.1.call-update) | async-done | bytes 65552 | tf_op jit(solution)/shard_map/while/body/eval_jaxpr/psum | solution.py:35
  776.4 68.6 %all-reduce.2.cloned.1.call-done = bf16[2,1,64,256]{3,2,1,0:T(8,128)(2,1)} async-done(((bf16[2,1,64,256]{3,2,1,0:T(8,128)(2,1)}), bf16[2,1,64,256]{3,2,1,0:T(8,128)(2,1)}) %all-reduce.2.cloned.1.call-update) | async-done | bytes 65552 | tf_op jit(solution)/shard_map/while/body/eval_jaxpr/psum | solution.py:35
  851.5 68.6 %all-reduce.2.cloned.1.call-done = bf16[2,1,64,256]{3,2,1,0:T(8,128)(2,1)} async-done(((bf16[2,1,64,256]{3,2,1,0:T(8,128)(2,1)}), bf16[2,1,64,256]{3,2,1,0:T(8,128)(2,1)}) %all-reduce.2.cloned.1.call-update) | async-done | bytes 65552 | tf_op jit(solution)/shard_map/while/body/eval_jaxpr/psum | solution.py:35
  926.7 68.6 %all-reduce.2.cloned.1.call-done = bf16[2,1,64,256]{3,2,1,0:T(8,128)(2,1)} async-done(((bf16[2,1,64,256]{3,2,1,0:T(8,128)(2,1)}), bf16[2,1,64,256]{3,2,1,0:T(8,128)(2,1)}) %all-reduce.2.cloned.1.call-update) | async-done | bytes 65552 | tf_op jit(solution)/shard_map/while/body/eval_jaxpr/psum | solution.py:35
  1001.9 68.6 %all-reduce.2.cloned.1.call-done = bf16[2,1,64,256]{3,2,1,0:T(8,128)(2,1)} async-done(((bf16[2,1,64,256]{3,2,1,0:T(8,128)(2,1)}), bf16[2,1,64,256]{3,2,1,0:T(8,128)(2,1)}) %all-reduce.2.cloned.1.call-update) | async-done | bytes 65552 | tf_op jit(solution)/shard_map/while/body/eval_jaxpr/psum | solution.py:35
  1077.0 68.6 %all-reduce.2.cloned.1.call-done = bf16[2,1,64,256]{3,2,1,0:T(8,128)(2,1)} async-done(((bf16[2,1,64,256]{3,2,1,0:T(8,128)(2,1)}), bf16[2,1,64,256]{3,2,1,0:T(8,128)(2,1)}) %all-reduce.2.cloned.1.call-update) | async-done | bytes 65552 | tf_op jit(solution)/shard_map/while/body/eval_jaxpr/psum | solution.py:35
  1152.2 68.6 %all-reduce.2.cloned.1.call-done = bf16[2,1,64,256]{3,2,1,0:T(8,128)(2,1)} async-done(((bf16[2,1,64,256]{3,2,1,0:T(8,128)(2,1)}), bf16[2,1,64,256]{3,2,1,0:T(8,128)(2,1)}) %all-reduce.2.cloned.1.call-update) | async-done | bytes 65552 | tf_op jit(solution)/shard_map/while/body/eval_jaxpr/psum | solution.py:35
  1222.2 3.3 reshape.132
  1225.5 2.4 copy.16
  1231.2 1.5 concatenate.17
  1235.5 1.7 gather_fusion.1
  1238.7 35.4 %while.40 = (s32[]{:T(128)}, bf16[2,8,64,256]{3,2,1,0:T(8,128)(2,1)}, bf16[2,24,64,256]{3,2,0,1:T(8,128)(2,1)}, s32[24]{0:T(128)S(1)}, s32[24]{0:T(128)S(1)}, /*index=5*/s32[]{:T(128)}, s32[]{:T(128)}, s32[]{:T(128)}, s32[]{:T(128)}) while((s32[]{:T(128)}, bf16[2,8,64,256]{3,2,1,0:T(8,128)(2,1)}, bf16[2,24,64,256]{3,2,0,1:T(8,128)(2,1)}, ...), condition=%wide.region_1.3_spmd, body=%wide.region_0.2_spmd.sunk | while | flops 1574141 | bytes 11015062 | solution.py:127
  1239.9 12.6 collective-permute-done
  1253.2 2.9 bitcast_select_fusion.3
  1256.9 12.9 collective-permute-done
  1270.4 2.9 bitcast_select_fusion.3
  1274.1 1.5 copy.10
  1275.6 2.9 concatenate.20
  1278.5 28.2 %maximum_bitcast_fusion = bf16[4,2,8,384,64]{4,0,3,2,1:T(4,128)(2,1)} fusion(bf16[2,8,192,4,64]{4,3,2,1,0:T(4,128)(2,1)} %concatenate.20, bf16[2,8,64,4,64]{4,3,2,1,0:T(4,128)(2,1)} %concatenate.19, bf16[2,8,64,4,64]{4,3,2,1,0:T(4,128)(2,1)} %concatenate.18, bf16[2,8,64,4,64]{4,3,2,1,0:T(4,128)(2,1)} %concatenate.17), kind=kLoop, calls=%fused_computation.38 | loop fusion | flops 4718592 | bytes 6291456 | tf_op jit(solution)/shard_map/transpose | solution.py:145
  1306.7 9.9 copy.12
  1316.6 30.7 %while.42 = (s32[]{:T(128)}, bf16[4,8,64,64]{3,2,1,0:T(8,128)(2,1)}, bf16[4,8,64,64]{3,2,1,0:T(8,128)(2,1)}, bf16[4,2,8,384,64]{3,4,2,1,0:T(8,128)(2,1)}, bf16[4...) while((s32[]{:T(128)}, bf16[4,8,64,64]{3,2,1,0:T(8,128)(2,1)}, ...), condition=%wide.region_10.12_spmd, body=%wide.region_5.11_spmd.sunk | while | flops 190708736 | bytes 16682657 | solution.py:152
  1320.7 1.6 fusion.40
  1322.2 2.0 fusion.41
  1328.3 1.6 fusion.40
  1329.9 2.0 fusion.41
  1336.0 1.6 fusion.40
  1337.6 2.0 fusion.41
  1343.7 1.6 fusion.40
  1345.3 2.0 fusion.41
  1350.5 9.9 reduce-scatter.2.cloned.1.call-done
  (187 shorter events, 95.0 us)
Async XLA Ops:
  7.4 1.2 copy-start
  7.4 2.7 copy-start.8
  10.5 6.0 copy-start.3
  11.4 11.0 copy-start.6
  11.4 11.7 copy-start.9
  11.4 1224.1 %collective-permute-start.3 = (bf16[2,8,64,256]{3,2,1,0:T(8,128)(2,1)}, bf16[2,8,64,256]{3,2,1,0:T(8,128)(2,1)}, u32[]{:S(2)}, u32[]{:S(2)}) collective-permute-start(bf16[2,8,64,256]{3,2,1,0:T(8,128)(2,1)} %pad_maximum_fusion.1), channel_id=1, source_target_pairs={{2,0},{4,2},{6,4},{8,6},{10,8},{12,10},{14,12},{0,14},{3,1},{5,3},... | collective-permute-start | bytes 1572872 | tf_op jit(solution)/shard_map/ppermute | solution.py:30
  17.2 1213.0 %collective-permute-start.1 = (bf16[2,64,256]{2,1,0:T(8,128)(2,1)}, bf16[2,64,256]{2,1,0:T(8,128)(2,1)S(1)}, u32[]{:S(2)}, u32[]{:S(2)}) collective-permute-start(bf16[2,64,256]{2,1,0:T(8,128)(2,1)} %get-tuple-element.311), channel_id=1, source_target_pairs={{0,2},{2,4},{4,6},{6,8},{8,10},{10,12},{12,14},{14,0},{1,3},{3,5},... | collective-permute-start | bytes 196616 | tf_op jit(solution)/shard_map/ppermute | solution.py:19
  17.2 1213.0 %collective-permute-start.2 = (bf16[2,64,256]{2,1,0:T(8,128)(2,1)S(1)}, bf16[2,64,256]{2,1,0:T(8,128)(2,1)}, u32[]{:S(2)}, u32[]{:S(2)}) collective-permute-start(bf16[2,64,256]{2,1,0:T(8,128)(2,1)S(1)} %get-tuple-element.312), channel_id=1, source_target_pairs={{2,0},{4,2},{6,4},{8,6},{10,8},{12,10},{14,12},{0,14},{3,1},{5,3},... | collective-permute-start | bytes 196616 | tf_op jit(solution)/shard_map/ppermute | solution.py:22
  23.2 70.1 %all-reduce.2.cloned.1.call-start = ((), (), s32[]{:S(2)}) async-start(), calls=%async_computation.2 | async-start | bytes 131072 | tf_op jit(solution)/shard_map/while/body/eval_jaxpr/psum | solution.py:35
  94.8 73.7 %all-reduce.2.cloned.1.call-start = ((), (), s32[]{:S(2)}) async-start(), calls=%async_computation.2 | async-start | bytes 131072 | tf_op jit(solution)/shard_map/while/body/eval_jaxpr/psum | solution.py:35
  170.0 73.7 %all-reduce.2.cloned.1.call-start = ((), (), s32[]{:S(2)}) async-start(), calls=%async_computation.2 | async-start | bytes 131072 | tf_op jit(solution)/shard_map/while/body/eval_jaxpr/psum | solution.py:35
  245.1 73.7 %all-reduce.2.cloned.1.call-start = ((), (), s32[]{:S(2)}) async-start(), calls=%async_computation.2 | async-start | bytes 131072 | tf_op jit(solution)/shard_map/while/body/eval_jaxpr/psum | solution.py:35
  320.3 73.7 %all-reduce.2.cloned.1.call-start = ((), (), s32[]{:S(2)}) async-start(), calls=%async_computation.2 | async-start | bytes 131072 | tf_op jit(solution)/shard_map/while/body/eval_jaxpr/psum | solution.py:35
  395.4 73.7 %all-reduce.2.cloned.1.call-start = ((), (), s32[]{:S(2)}) async-start(), calls=%async_computation.2 | async-start | bytes 131072 | tf_op jit(solution)/shard_map/while/body/eval_jaxpr/psum | solution.py:35
  470.6 73.7 %all-reduce.2.cloned.1.call-start = ((), (), s32[]{:S(2)}) async-start(), calls=%async_computation.2 | async-start | bytes 131072 | tf_op jit(solution)/shard_map/while/body/eval_jaxpr/psum | solution.py:35
  545.7 73.7 %all-reduce.2.cloned.1.call-start = ((), (), s32[]{:S(2)}) async-start(), calls=%async_computation.2 | async-start | bytes 131072 | tf_op jit(solution)/shard_map/while/body/eval_jaxpr/psum | solution.py:35
  620.9 73.7 %all-reduce.2.cloned.1.call-start = ((), (), s32[]{:S(2)}) async-start(), calls=%async_computation.2 | async-start | bytes 131072 | tf_op jit(solution)/shard_map/while/body/eval_jaxpr/psum | solution.py:35
  696.1 73.7 %all-reduce.2.cloned.1.call-start = ((), (), s32[]{:S(2)}) async-start(), calls=%async_computation.2 | async-start | bytes 131072 | tf_op jit(solution)/shard_map/while/body/eval_jaxpr/psum | solution.py:35
  771.2 73.7 %all-reduce.2.cloned.1.call-start = ((), (), s32[]{:S(2)}) async-start(), calls=%async_computation.2 | async-start | bytes 131072 | tf_op jit(solution)/shard_map/while/body/eval_jaxpr/psum | solution.py:35
  846.4 73.7 %all-reduce.2.cloned.1.call-start = ((), (), s32[]{:S(2)}) async-start(), calls=%async_computation.2 | async-start | bytes 131072 | tf_op jit(solution)/shard_map/while/body/eval_jaxpr/psum | solution.py:35
  921.6 73.7 %all-reduce.2.cloned.1.call-start = ((), (), s32[]{:S(2)}) async-start(), calls=%async_computation.2 | async-start | bytes 131072 | tf_op jit(solution)/shard_map/while/body/eval_jaxpr/psum | solution.py:35
  996.7 73.7 %all-reduce.2.cloned.1.call-start = ((), (), s32[]{:S(2)}) async-start(), calls=%async_computation.2 | async-start | bytes 131072 | tf_op jit(solution)/shard_map/while/body/eval_jaxpr/psum | solution.py:35
  1071.9 73.7 %all-reduce.2.cloned.1.call-start = ((), (), s32[]{:S(2)}) async-start(), calls=%async_computation.2 | async-start | bytes 131072 | tf_op jit(solution)/shard_map/while/body/eval_jaxpr/psum | solution.py:35
  1147.0 73.7 %all-reduce.2.cloned.1.call-start = ((), (), s32[]{:S(2)}) async-start(), calls=%async_computation.2 | async-start | bytes 131072 | tf_op jit(solution)/shard_map/while/body/eval_jaxpr/psum | solution.py:35
  1222.2 138.2 %reduce-scatter.2.cloned.1.call-start = ((), (), s32[]{:S(2)}) async-start(), calls=%async_computation.1 | async-start | bytes 1572864 | tf_op jit(solution)/shard_map/reduce_scatter | solution.py:155
  1227.9 2.2 copy-start.7
  1227.9 2.2 copy-start.4
  1238.7 13.8 %collective-permute-start = (bf16[2,8,64,256]{3,2,1,0:T(8,128)(2,1)}, bf16[2,8,64,256]{3,2,1,0:T(8,128)(2,1)S(1)}, u32[]{:S(2)}, u32[]{:S(2)}) collective-permute-start(bf16[2,8,64,256]{3,2,1,0:T(8,128)(2,1)} %get-tuple-element.432), channel_id=1, source_target_pairs={{14,0},{0,2},{2,4},{4,6},{6,8},{8,10},{10,12},{12,14},{15,1},{1,3}... | collective-permute-start | bytes 1572872 | tf_op jit(solution)/shard_map/while/body/eval_jaxpr/ppermute | solution.py:30
  1256.9 12.9 collective-permute-start
  1319.4 0.9 copy-start.1
  1320.6 1.6 copy-start.2
  1327.1 0.9 copy-start.1
  1328.3 1.6 copy-start.2
  1334.8 0.9 copy-start.1
  1336.0 1.6 copy-start.2
  1342.5 0.9 copy-start.1
  1343.7 1.6 copy-start.2
  1347.3 1.7 copy-start.5
Sparse Core Ops, SparseCore 0:
  28.5 64.7 all-reduce.1
  100.1 68.3 all-reduce.1
  175.2 68.3 all-reduce.1
  250.4 68.3 all-reduce.1
  325.5 68.3 all-reduce.1
  400.7 68.3 all-reduce.1
  475.8 68.3 all-reduce.1
  551.0 68.3 all-reduce.1
  626.2 68.3 all-reduce.1
  701.3 68.3 all-reduce.1
  776.5 68.3 all-reduce.1
  851.7 68.3 all-reduce.1
  926.8 68.3 all-reduce.1
  1002.0 68.3 all-reduce.1
  1077.1 68.3 all-reduce.1
  1152.3 68.3 all-reduce.1
Sparse Core Ops, SparseCore 1:
  1350.6 9.7 reduce-scatter.1
where the time goes:
time: 1370 us
  waiting for transfers between devices  1130 us (82%)
  local copies, waits for them, and re-layouts  78.1 us (6%)
  other arithmetic  65.5 us (5%)
  loops' own time  39.8 us (3%)
  matrix products  30.2 us (2%)
  between operations  14.6 us (1%)
    psum x16, waiting for transfers between devices, broadcast(): return lax.psum(jnp.where(mine, shard, jnp.zeros_like(shard)), axis)  1090 us
    another operation x1, loops' own time, on_device(): lax.fori_loop(0, global_count, fetch_global, jnp.zeros((2, global_count,...  39.4 us
    transpose x1, other arithmetic, on_device(): local_block_pair.reshape(2, blk_count, -1, head_count, HEAD_DIM)  28.2 us
  transfers between devices with their start and end apart: 22, of which 19 were waited for; matrix products, arithmetic and copies ran while one was open for 6% of the time, Pallas kernels for 0%

commit v1 on v0

--- a/solution.py
+++ b/solution.py
@@ -3,11 +3,14 @@
 import jax
 import jax.numpy as jnp
 from jax import lax
+from jax.experimental import pallas as pl
+from jax.experimental.pallas import tpu as pltpu
 from jax.sharding import PartitionSpec as P
 
 HEAD_DIM = 64
 BLOCK = 64
 RAND = 3
+MESH = pl.DeviceIdType.MESH
 
 
 def padded_2(block, sides, width):
@@ -157,9 +160,286 @@
     )
 
 
+def route_kernel(rand_ref, gid_ref, tok_ref, wqkv_ref, wout_ref, out_ref,
+                 krow, vrow, kz, vz, q_ref, gk, gv, near_k, near_v, far_k, far_v,
+                 nsend_k, nsend_v, fsend_k, fsend_v, wfull, att,
+                 xs, xr, zs, zr, ns, nr, fs, fr, gs, gr, ws, wr, hs, hr):
+    rows = tok_ref.shape[0]
+    feats = wqkv_ref.shape[2]
+    half_out = out_ref.shape[1]
+    blocks = rows // BLOCK
+    pair = 2 * blocks
+    heads = feats // HEAD_DIM
+    slots = gid_ref.shape[0]
+    mine = slots // 2
+    me = lax.axis_index("seq")
+    core = lax.axis_index("head")
+    cycle = lax.axis_size("seq")
+    lines = cycle // 2
+    z = me // 2
+    x = me % 2
+    partner = z * 2 + (1 - x)
+    z_next = ((z + 1) % lines) * 2 + x
+    z_prev = ((z + lines - 1) % lines) * 2 + x
+    to_near = ((z + 1 + (lines - 2) * x) % lines) * 2 + x
+    side = (z * 2) // lines
+    ahead = z + 1 - 2 * side
+    behind = (z + lines - 1 + 2 * side) % lines
+    inner = jnp.logical_and(z > 0, z < lines - 1)
+    fwd_dev = ahead * 2 + x
+    back_dev = behind * 2 + x
+
+    barrier = pltpu.get_barrier_semaphore()
+    for who in ({"seq": partner}, {"seq": z_next}, {"seq": z_prev}, {"head": 1 - core}):
+        pl.semaphore_signal(barrier, inc=1, device_id=who, device_id_type=MESH)
+
+    def remote(src, dst, ssem, rsem, who):
+        return pltpu.make_async_remote_copy(
+            src_ref=src, dst_ref=dst, send_sem=ssem, recv_sem=rsem,
+            device_id=who, device_id_type=MESH)
+
+    here = pl.ds(pl.multiple_of(x * rows, rows), rows)
+    there = pl.ds(pl.multiple_of((1 - x) * rows, rows), rows)
+
+    def project(index):
+        return jnp.dot(tok_ref[...], wqkv_ref[index],
+                       preferred_element_type=jnp.float32).astype(jnp.bfloat16)
+
+    krow[here, :] = project(1)
+    pl.semaphore_wait(barrier, 4)
+    send_x = [remote(buf.at[here], buf.at[here], xs.at[i], xr.at[i], {"seq": partner})
+              for i, buf in enumerate((krow, vrow))]
+    got_x = [remote(buf.at[there], buf.at[there], xs.at[i], xr.at[i], {"seq": partner})
+             for i, buf in enumerate((krow, vrow))]
+    send_x[0].start()
+    vrow[here, :] = project(2)
+    send_x[1].start()
+    wmine = pl.ds(pl.multiple_of(core * feats, feats), feats)
+    wother = pl.ds(pl.multiple_of((1 - core) * feats, feats), feats)
+    send_w = remote(
+        wout_ref.at[:, pl.ds(pl.multiple_of((1 - core) * half_out, half_out), half_out)],
+        wfull.at[wmine], ws.at[0], wr.at[0], {"head": 1 - core})
+    send_w.start()
+    wfull[wmine, :] = wout_ref[:, pl.ds(pl.multiple_of(core * half_out, half_out), half_out)]
+    q_ref[...] = project(0)
+
+    near = (near_k, near_v)
+    far = (far_k, far_v)
+    nsend = (nsend_k, nsend_v)
+    fsend = (fsend_k, fsend_v)
+    row = (krow, vrow)
+    zbuf = (kz, vz)
+    gbuf = (gk, gv)
+
+    def near_copy(kind, j, crossing):
+        part = pl.ds(j * BLOCK, BLOCK)
+        n = kind * mine + j
+        dst, sem = (far, fr) if crossing else (near, nr)
+        return remote(nsend[kind].at[part], dst[kind].at[part], ns.at[n], sem.at[n],
+                      {"seq": fwd_dev})
+
+    def far_copy(kind, j):
+        part = pl.ds(j * BLOCK, BLOCK)
+        n = kind * mine + j
+        return remote(fsend[kind].at[part], far[kind].at[part], fs.at[n], fr.at[n],
+                      {"seq": back_dev})
+
+    def owner(j):
+        gid = gid_ref[x * mine + j]
+        return lax.div(gid, pair), lax.rem(gid, pair)
+
+    def step_near(kind, j):
+        part = pl.ds(j * BLOCK, BLOCK)
+        line, within = owner(j)
+        own = row[kind][pl.ds(within * BLOCK, BLOCK), :]
+
+        @pl.when(inner)
+        def _():
+            near_copy(kind, j, False).wait_recv()
+            nsend[kind][part, :] = jnp.where(line == z, own, near[kind][part, :])
+            near_copy(kind, j, True).start()
+
+        @pl.when(jnp.logical_not(inner))
+        def _():
+            nsend[kind][part, :] = own
+            near_copy(kind, j, False).start()
+
+    def g_copy(kind, j):
+        spot = pl.ds(pl.multiple_of((x * mine + j) * BLOCK, BLOCK), BLOCK)
+        n = kind * mine + j
+        return remote(gbuf[kind].at[spot], gbuf[kind].at[spot], gs.at[n], gr.at[n],
+                      {"seq": partner})
+
+    def step_far(kind, j):
+        part = pl.ds(j * BLOCK, BLOCK)
+        spot = pl.ds(pl.multiple_of((x * mine + j) * BLOCK, BLOCK), BLOCK)
+        line, within = owner(j)
+        own = row[kind][pl.ds(within * BLOCK, BLOCK), :]
+        far_copy(kind, j).wait_recv()
+        arrived = far[kind][part, :]
+
+        @pl.when(inner)
+        def _():
+            fsend[kind][part, :] = jnp.where(line == z, own, arrived)
+            far_copy(kind, j).start()
+            before = jnp.where(side == 0, line < z, line > z)
+            gbuf[kind][spot, :] = jnp.where(
+                line == z, own, jnp.where(before, near[kind][part, :], arrived))
+
+        @pl.when(jnp.logical_not(inner))
+        def _():
+            gbuf[kind][spot, :] = jnp.where(line == z, own, arrived)
+
+        g_copy(kind, j).start()
+
+    send_z = [remote(row[i].at[there], zbuf[i], zs.at[i], zr.at[i], {"seq": to_near})
+              for i in range(2)]
+
+    lag = 3
+    total = 2 * mine
+    for t in range(total + lag):
+        if t < total:
+            kind, j = t // mine, t % mine
+            if j == 0:
+                got_x[kind].wait_recv()
+            step_near(kind, j)
+            if j == mine - 1:
+                send_z[kind].start()
+        if t >= lag:
+            u = t - lag
+            step_far(u // mine, u % mine)
+
+    for kind in range(2):
+        for j in range(mine):
+            n = kind * mine + j
+            spot = pl.ds(pl.multiple_of(((1 - x) * mine + j) * BLOCK, BLOCK), BLOCK)
+            remote(gbuf[kind].at[spot], gbuf[kind].at[spot], gs.at[n], gr.at[n],
+                   {"seq": partner}).wait_recv()
+    for kind in range(2):
+        send_z[kind].wait_recv()
+
+    lane_head = lax.broadcasted_iota(jnp.int32, (BLOCK, feats), 1) // HEAD_DIM
+    masks = [(lane_head == h).astype(jnp.float32) for h in range(heads)]
+    masks16 = [m.astype(jnp.bfloat16) for m in masks]
+    factor = math.log2(math.e) / math.sqrt(HEAD_DIM)
+    doc_blocks = cycle * blocks
+
+    def fetch(bufs, e):
+        place = e - pair * z
+        inside = jnp.logical_and(place >= 0, place < pair)
+        place = jnp.clip(place, 0, pair - 1)
+        a = bufs[0][pl.ds(place * BLOCK, BLOCK), :]
+        b = bufs[1][pl.ds(lax.rem(e, blocks) * BLOCK, BLOCK), :]
+        return jnp.where(inside, a, b)
+
+    def att_copy(b):
+        spot = pl.ds(pl.multiple_of(b * BLOCK, BLOCK), BLOCK)
+        return remote(att.at[core, spot], att.at[core, spot], hs.at[b], hr.at[b],
+                      {"head": 1 - core})
+
+    def one_block(b, carry):
+        spot = pl.ds(pl.multiple_of(b * BLOCK, BLOCK), BLOCK)
+        q = q_ref[spot, :]
+        stacked = jnp.concatenate([q * m for m in masks16], axis=0)
+        mid = me * blocks + b
+        picks = [lax.rem(mid + doc_blocks - 1, doc_blocks), mid,
+                 lax.rem(mid + 1, doc_blocks)] + [rand_ref[b, i] for i in range(RAND)]
+        kloc = jnp.concatenate([fetch((krow, kz), e) for e in picks], axis=0)
+        vloc = jnp.concatenate([fetch((vrow, vz), e) for e in picks], axis=0)
+        dims = (((1,), (1,)), ((), ()))
+        sl = lax.dot_general(stacked, kloc, dims, preferred_element_type=jnp.float32)
+        sg = lax.dot_general(stacked, gk[...], dims, preferred_element_type=jnp.float32)
+        top = jnp.maximum(jnp.max(sl, axis=1, keepdims=True), jnp.max(sg, axis=1, keepdims=True))
+        el = jnp.exp2((sl - top) * factor)
+        eg = jnp.exp2((sg - top) * factor)
+        norm = jnp.sum(el, axis=1, keepdims=True) + jnp.sum(eg, axis=1, keepdims=True)
+        o = jnp.dot(el.astype(jnp.bfloat16), vloc, preferred_element_type=jnp.float32)
+        o += jnp.dot(eg.astype(jnp.bfloat16), gv[...], preferred_element_type=jnp.float32)
+        o = o / norm
+        merged = o[0:BLOCK] * masks[0]
+        for h in range(1, heads):
+            merged += o[h * BLOCK:(h + 1) * BLOCK] * masks[h]
+        att[core, spot, :] = merged.astype(jnp.bfloat16)
+        att_copy(b).start()
+        return carry
+
+    lax.fori_loop(0, blocks, one_block, 0)
+
+    remote(wout_ref.at[:, pl.ds(0, half_out)], wfull.at[wother], ws.at[0], wr.at[0],
+           {"head": 1 - core}).wait_recv()
+    acc = jnp.dot(att[core], wfull[wmine, :], preferred_element_type=jnp.float32)
+
+    def other_in(b, carry):
+        spot = pl.ds(pl.multiple_of(b * BLOCK, BLOCK), BLOCK)
+        remote(att.at[1 - core, spot], att.at[1 - core, spot], hs.at[b], hr.at[b],
+               {"head": 1 - core}).wait_recv()
+        return carry
+
+    lax.fori_loop(0, blocks, other_in, 0)
+    acc += jnp.dot(att[1 - core], wfull[wother, :], preferred_element_type=jnp.float32)
+    out_ref[...] = acc.astype(jnp.bfloat16)
+
+    for kind in range(2):
+        send_x[kind].wait_send()
+        send_z[kind].wait_send()
+        for j in range(mine):
+            near_copy(kind, j, False).wait_send()
+            g_copy(kind, j).wait_send()
+    send_w.wait_send()
+
+    @pl.when(inner)
+    def _():
+        for kind in range(2):
+            for j in range(mine):
+                far_copy(kind, j).wait_send()
+
+    def sent(b, carry):
+        att_copy(b).wait_send()
+        return carry
+
+    lax.fori_loop(0, blocks, sent, 0)
+
+
+def routed(tokens, w_qkv, w_out, random_blocks, global_ids):
+    rows = tokens.shape[0]
+    feats = w_qkv.shape[2]
+    width = w_out.shape[1]
+    heads_axis = lax.axis_size("head")
+    slots = global_ids.shape[0]
+    blocks = rows // BLOCK
+    mine = slots // 2
+    vm = pl.BlockSpec(memory_space=pltpu.VMEM)
+    sm = pl.BlockSpec(memory_space=pltpu.SMEM)
+    bf = jnp.bfloat16
+    chain = pltpu.VMEM((mine * BLOCK, feats), bf)
+    dma = pltpu.SemaphoreType.DMA
+    return pl.pallas_call(
+        route_kernel,
+        out_shape=jax.ShapeDtypeStruct((rows, width // heads_axis), bf),
+        in_specs=[sm, sm, vm, vm, vm],
+        out_specs=vm,
+        scratch_shapes=[
+            pltpu.VMEM((2 * rows, feats), bf), pltpu.VMEM((2 * rows, feats), bf),
+            pltpu.VMEM((rows, feats), bf), pltpu.VMEM((rows, feats), bf),
+            pltpu.VMEM((rows, feats), bf),
+            pltpu.VMEM((slots * BLOCK, feats), bf), pltpu.VMEM((slots * BLOCK, feats), bf),
+            chain, chain, chain, chain, chain, chain, chain, chain,
+            pltpu.VMEM((heads_axis * feats, width // heads_axis), bf),
+            pltpu.VMEM((heads_axis, rows, feats), bf),
+            dma((2,)), dma((2,)), dma((2,)), dma((2,)),
+            dma((slots,)), dma((slots,)), dma((slots,)), dma((slots,)),
+            dma((slots,)), dma((slots,)), dma((1,)), dma((1,)),
+            dma((blocks,)), dma((blocks,)),
+        ],
+        compiler_params=pltpu.CompilerParams(
+            collective_id=0, has_side_effects=True, vmem_limit_bytes=48 * 1024 * 1024),
+    )(random_blocks, global_ids, tokens, w_qkv, w_out)
+
+
 def solution(mesh):
+    small = mesh.shape["seq"] == 8 and mesh.shape["head"] == 2
     return jax.shard_map(
-        on_device,
+        routed if small else on_device,
         mesh=mesh,
         in_specs=(
             P(("groups", "seq"), None),

time: 1370 us -> 122 us (0.09)
  waiting for transfers between devices: 1130 us -> 0 us
  Pallas kernels: 0 us -> 116 us
  local copies, waits for them, and re-layouts: 78.1 us -> 5.88 us
  other arithmetic: 65.5 us -> 0 us
  loops' own time: 39.8 us -> 0 us
  matrix products: 30.2 us -> 0 us
  between operations: 14.6 us -> 0.01 us
    psum x16 -> x0, waiting for transfers between devices: 1090 us -> none  [broadcast(): return lax.psum(jnp.where(mine, shard, jnp.zeros_like(shard)), axis)]
    pallas_call x0 -> x1, Pallas kernels: none -> 116 us  [routed(): pl.pallas_call(route_kernel, out_shape=jax.ShapeDtypeStruct((rows, width...]
    another operation x3 -> x0, loops' own time: 39.8 us -> none  [the longest x1 39.4 us: on_device(): lax.fori_loop(0, global_count, fetch_global, jnp.zeros((2, global_count,...]
    select_n x23 -> x0, other arithmetic: 31.5 us -> none  [the longest x16 23.7 us: broadcast(): return lax.psum(jnp.where(mine, shard, jnp.zeros_like(shard)), axis)]
    dot_general x20 -> x0, matrix products: 30.2 us -> none  [the longest x4 8.05 us: attend_head(): jnp.einsum('onw,owz->onz', local_attention_weights, local_block_pair[1],...]
    transpose x1 -> x0, other arithmetic: 28.2 us -> none  [on_device(): local_block_pair.reshape(2, blk_count, -1, head_count, HEAD_DIM)]
    ppermute x5 -> x0, waiting for transfers between devices: 25.5 us -> none  [the longest x3 25.5 us: passed_along(): return lax.ppermute(block, axis, route)]
    dynamic_update_slice x16 -> x0, local copies, waits for them, and re-layouts: 23.5 us -> none  [fetch_global(): lax.dynamic_update_index_in_dim(gathered, arrived, slot_index, axis=1)]
  transfers between devices with their start and end apart: 22 -> 0, of which waited for: 19 -> 0; matrix products, arithmetic and copies ran while one was open for 6% -> 0% of each run, Pallas kernels for 0% -> 0%
where the time goes in v1:
time: 122 us
  Pallas kernels  116 us (95%)
  local copies, waits for them, and re-layouts  5.88 us (5%)
    pallas_call x1, Pallas kernels, routed(): pl.pallas_call(route_kernel, out_shape=jax.ShapeDtypeStruct((rows, width...  116 us
    unnamed x10, local copies, waits for them, and re-layouts  5.88 us

profile of v1, /device:TPU:1, one launch (start us, length us, event | category | flops | bytes accessed | tf_op | source)
XLA Modules:
  0.0 121.6 jit_solution(13674617459079097384)
XLA Ops:
  0.0 0.8 copy.6.rand_ref
  0.8 0.0 copy-start
  0.8 1.4 %copy-done = bf16[3,1024,256]{2,1,0:T(8,128)(2,1)S(1)} copy-done((bf16[3,1024,256]{2,1,0:T(8,128)(2,1)S(1)}, bf16[3,1024,256]{2,1,0:T(8,128)(2,1)}, u32[]{:S(2)}) %copy-start) | copy-done | bytes 1572888
  2.2 0.0 copy-start.1
  2.2 1.2 %copy-done.1 = bf16[512,1024]{1,0:T(8,128)(2,1)S(1)} copy-done((bf16[512,1024]{1,0:T(8,128)(2,1)S(1)}, bf16[512,1024]{1,0:T(8,128)(2,1)}, u32[]{:S(2)}) %copy-start.1) | copy-done | bytes 1048600
  3.4 0.0 copy-start.2
  3.4 1.0 copy-done.2
  4.4 0.0 copy-start.3
  4.4 0.7 copy-done.3
  5.1 115.7 %shard_map.55 = bf16[512,512]{1,0:T(8,128)(2,1)S(1)} custom-call(s32[8,3]{1,0:T(8,128)S(1)} %copy.6.rand_ref, s32[16]{0:T(128)S(1)} %copy-done.3, bf16[512,1024]{1,0:T(8,128)(2,1)S(1)} %copy-done.1, bf16[3,1024,256]{2,1,0:T(8,128)(2,1)S(1)} %copy-done, bf16[256,1024]{1,0:T(8,128)(2,1)S(1)} %copy-done.2), custom_call_target="tpu_custom_call" | custom-call | tf_op jit(solution)/shard_map/pallas_call | solution.py:416
  120.8 0.8 copy.8
Async XLA Ops:
  0.8 1.4 %copy-start = (bf16[3,1024,256]{2,1,0:T(8,128)(2,1)S(1)}, bf16[3,1024,256]{2,1,0:T(8,128)(2,1)}, u32[]{:S(2)}) copy-start(bf16[3,1024,256]{2,1,0:T(8,128)(2,1)} %wqkv_ref.1) | copy-start | bytes 4718596
  2.2 1.2 %copy-start.1 = (bf16[512,1024]{1,0:T(8,128)(2,1)S(1)}, bf16[512,1024]{1,0:T(8,128)(2,1)}, u32[]{:S(2)}) copy-start(bf16[512,1024]{1,0:T(8,128)(2,1)} %tok_ref.1) | copy-start | bytes 3145732
  3.4 1.0 copy-start.2
  4.4 0.7 copy-start.3

commit v2 on v1

--- a/solution.py
+++ b/solution.py
@@ -295,19 +295,31 @@
     send_z = [remote(row[i].at[there], zbuf[i], zs.at[i], zr.at[i], {"seq": to_near})
               for i in range(2)]
 
-    lag = 3
-    total = 2 * mine
-    for t in range(total + lag):
-        if t < total:
-            kind, j = t // mine, t % mine
-            if j == 0:
-                got_x[kind].wait_recv()
-            step_near(kind, j)
-            if j == mine - 1:
-                send_z[kind].start()
-        if t >= lag:
-            u = t - lag
-            step_far(u // mine, u % mine)
+    got_x[0].wait_recv()
+    for j in range(mine):
+        step_near(0, j)
+
+    @pl.when(jnp.logical_not(inner))
+    def _():
+        got_x[1].wait_recv()
+        for j in range(mine):
+            step_near(1, j)
+        send_z[0].start()
+        send_z[1].start()
+        for kind in range(2):
+            for j in range(mine):
+                step_far(kind, j)
+
+    @pl.when(inner)
+    def _():
+        got_x[1].wait_recv()
+        send_z[0].start()
+        for j in range(mine):
+            step_near(1, j)
+            step_far(0, j)
+        send_z[1].start()
+        for j in range(mine):
+            step_far(1, j)
 
     for kind in range(2):
         for j in range(mine):

time: 122 us -> 64.4 us (0.53)
  the two profiles are of different devices: /device:TPU:1 before, /device:TPU:3 now
where the time goes in v2:
time: 64.4 us; the launch traced here: 64.1 us
  Pallas kernels  58.2 us (90%)
  local copies, waits for them, and re-layouts  5.88 us (9%)
    pallas_call x1, Pallas kernels, routed(): pl.pallas_call(route_kernel, out_shape=jax.ShapeDtypeStruct((rows, width...  58.2 us
    unnamed x10, local copies, waits for them, and re-layouts  5.88 us

profile of v2, /device:TPU:3, one launch (start us, length us, event | category | flops | bytes accessed | tf_op | source)
XLA Modules:
  0.0 64.1 jit_solution(5780702993520609866)
XLA Ops:
  0.0 0.8 %copy.6.rand_ref = s32[8,3]{1,0:T(8,128)S(1)} copy(s32[8,3]{0,1:T(4,128)} %param.8) | data formatting | bytes 192 | tf_op args[3]
  0.8 0.0 copy-start
  0.8 1.4 %copy-done = bf16[3,1024,256]{2,1,0:T(8,128)(2,1)S(1)} copy-done((bf16[3,1024,256]{2,1,0:T(8,128)(2,1)S(1)}, bf16[3,1024,256]{2,1,0:T(8,128)(2,1)}, u32[]{:S(2)}) %copy-start) | copy-done | bytes 1572888
  2.2 0.0 copy-start.1
  2.2 1.2 %copy-done.1 = bf16[512,1024]{1,0:T(8,128)(2,1)S(1)} copy-done((bf16[512,1024]{1,0:T(8,128)(2,1)S(1)}, bf16[512,1024]{1,0:T(8,128)(2,1)}, u32[]{:S(2)}) %copy-start.1) | copy-done | bytes 1048600
  3.4 0.0 copy-start.2
  3.4 1.0 %copy-done.2 = bf16[256,1024]{1,0:T(8,128)(2,1)S(1)} copy-done((bf16[256,1024]{1,0:T(8,128)(2,1)S(1)}, bf16[256,1024]{1,0:T(8,128)(2,1)}, u32[]{:S(2)}) %copy-start.2) | copy-done | bytes 524312
  4.4 0.0 copy-start.3
  4.4 0.7 %copy-done.3 = s32[16]{0:T(128)S(1)} copy-done((s32[16]{0:T(128)S(1)}, s32[16]{0:T(128)}, u32[]{:S(2)}) %copy-start.3) | copy-done | bytes 88
  5.1 58.2 %shard_map.55 = bf16[512,512]{1,0:T(8,128)(2,1)S(1)} custom-call(s32[8,3]{1,0:T(8,128)S(1)} %copy.6.rand_ref, s32[16]{0:T(128)S(1)} %copy-done.3, bf16[512,1024]{1,0:T(8,128)(2,1)S(1)} %copy-done.1, bf16[3,1024,256]{2,1,0:T(8,128)(2,1)S(1)} %copy-done, bf16[256,1024]{1,0:T(8,128)(2,1)S(1)} %copy-done.2), custom_call_target="tpu_custom_call" | custom-call | tf_op jit(solution)/shard_map/pallas_call | solution.py:428
  63.3 0.8 %copy.8 = bf16[512,512]{1,0:T(8,128)(2,1)} copy(bf16[512,512]{1,0:T(8,128)(2,1)S(1)} %shard_map.55) | data formatting | bytes 1048576
Async XLA Ops:
  0.8 1.4 %copy-start = (bf16[3,1024,256]{2,1,0:T(8,128)(2,1)S(1)}, bf16[3,1024,256]{2,1,0:T(8,128)(2,1)}, u32[]{:S(2)}) copy-start(bf16[3,1024,256]{2,1,0:T(8,128)(2,1)} %wqkv_ref.1) | copy-start | bytes 4718596
  2.2 1.2 %copy-start.1 = (bf16[512,1024]{1,0:T(8,128)(2,1)S(1)}, bf16[512,1024]{1,0:T(8,128)(2,1)}, u32[]{:S(2)}) copy-start(bf16[512,1024]{1,0:T(8,128)(2,1)} %tok_ref.1) | copy-start | bytes 3145732
  3.4 1.0 %copy-start.2 = (bf16[256,1024]{1,0:T(8,128)(2,1)S(1)}, bf16[256,1024]{1,0:T(8,128)(2,1)}, u32[]{:S(2)}) copy-start(bf16[256,1024]{1,0:T(8,128)(2,1)} %wout_ref.1) | copy-start | bytes 1572868
  4.4 0.7 %copy-start.3 = (s32[16]{0:T(128)S(1)}, s32[16]{0:T(128)}, u32[]{:S(2)}) copy-start(s32[16]{0:T(128)} %gid_ref.1) | copy-start | bytes 196

commit v3 on v2

--- a/solution.py
+++ b/solution.py
@@ -160,10 +160,18 @@
     )
 
 
-def route_kernel(rand_ref, gid_ref, tok_ref, wqkv_ref, wout_ref, out_ref,
+def route_kernel(rand_hbm, gid_hbm, tok_hbm, wqkv_hbm, wout_hbm, out_ref,
+                 rand_ref, gid_ref, tok_ref, wqkv_ref, wout_ref, ls,
                  krow, vrow, kz, vz, q_ref, gk, gv, near_k, near_v, far_k, far_v,
                  nsend_k, nsend_v, fsend_k, fsend_v, wfull, att,
                  xs, xr, zs, zr, ns, nr, fs, fr, gs, gr, ws, wr, hs, hr):
+    load_tok = pltpu.make_async_copy(tok_hbm, tok_ref, ls.at[0])
+    load_w = [pltpu.make_async_copy(wqkv_hbm.at[i], wqkv_ref.at[i], ls.at[1 + i]) for i in range(3)]
+    load_o = pltpu.make_async_copy(wout_hbm, wout_ref, ls.at[4])
+    load_r = pltpu.make_async_copy(rand_hbm, rand_ref, ls.at[5])
+    load_g = pltpu.make_async_copy(gid_hbm, gid_ref, ls.at[6])
+    for load in (load_w[1], load_tok, load_w[2], load_g, load_o, load_w[0], load_r):
+        load.start()
     rows = tok_ref.shape[0]
     feats = wqkv_ref.shape[2]
     half_out = out_ref.shape[1]
@@ -205,6 +213,8 @@
         return jnp.dot(tok_ref[...], wqkv_ref[index],
                        preferred_element_type=jnp.float32).astype(jnp.bfloat16)
 
+    load_tok.wait()
+    load_w[1].wait()
     krow[here, :] = project(1)
     pl.semaphore_wait(barrier, 4)
     send_x = [remote(buf.at[here], buf.at[here], xs.at[i], xr.at[i], {"seq": partner})
@@ -212,8 +222,10 @@
     got_x = [remote(buf.at[there], buf.at[there], xs.at[i], xr.at[i], {"seq": partner})
              for i, buf in enumerate((krow, vrow))]
     send_x[0].start()
+    load_w[2].wait()
     vrow[here, :] = project(2)
     send_x[1].start()
+    load_o.wait()
     wmine = pl.ds(pl.multiple_of(core * feats, feats), feats)
     wother = pl.ds(pl.multiple_of((1 - core) * feats, feats), feats)
     send_w = remote(
@@ -221,6 +233,9 @@
         wfull.at[wmine], ws.at[0], wr.at[0], {"head": 1 - core})
     send_w.start()
     wfull[wmine, :] = wout_ref[:, pl.ds(pl.multiple_of(core * half_out, half_out), half_out)]
+    load_w[0].wait()
+    load_r.wait()
+    load_g.wait()
     q_ref[...] = project(0)
 
     near = (near_k, near_v)
@@ -296,15 +311,20 @@
               for i in range(2)]
 
     got_x[0].wait_recv()
+
+    @pl.when(inner)
+    def _():
+        send_z[0].start()
+
     for j in range(mine):
         step_near(0, j)
 
     @pl.when(jnp.logical_not(inner))
     def _():
+        send_z[0].start()
         got_x[1].wait_recv()
         for j in range(mine):
             step_near(1, j)
-        send_z[0].start()
         send_z[1].start()
         for kind in range(2):
             for j in range(mine):
@@ -313,11 +333,10 @@
     @pl.when(inner)
     def _():
         got_x[1].wait_recv()
-        send_z[0].start()
+        send_z[1].start()
         for j in range(mine):
             step_near(1, j)
             step_far(0, j)
-        send_z[1].start()
         for j in range(mine):
             step_far(1, j)
 
@@ -355,7 +374,7 @@
         stacked = jnp.concatenate([q * m for m in masks16], axis=0)
         mid = me * blocks + b
         picks = [lax.rem(mid + doc_blocks - 1, doc_blocks), mid,
-                 lax.rem(mid + 1, doc_blocks)] + [rand_ref[b, i] for i in range(RAND)]
+                 lax.rem(mid + 1, doc_blocks)] + [rand_ref[i, b] for i in range(RAND)]
         kloc = jnp.concatenate([fetch((krow, kz), e) for e in picks], axis=0)
         vloc = jnp.concatenate([fetch((vrow, vz), e) for e in picks], axis=0)
         dims = (((1,), (1,)), ((), ()))
@@ -421,16 +440,19 @@
     blocks = rows // BLOCK
     mine = slots // 2
     vm = pl.BlockSpec(memory_space=pltpu.VMEM)
-    sm = pl.BlockSpec(memory_space=pltpu.SMEM)
+    hb = pl.BlockSpec(memory_space=pltpu.HBM)
     bf = jnp.bfloat16
     chain = pltpu.VMEM((mine * BLOCK, feats), bf)
     dma = pltpu.SemaphoreType.DMA
     return pl.pallas_call(
         route_kernel,
         out_shape=jax.ShapeDtypeStruct((rows, width // heads_axis), bf),
-        in_specs=[sm, sm, vm, vm, vm],
+        in_specs=[hb, hb, hb, hb, hb],
         out_specs=vm,
         scratch_shapes=[
+            pltpu.SMEM(random_blocks.shape[::-1], jnp.int32), pltpu.SMEM(global_ids.shape, jnp.int32),
+            pltpu.VMEM(tokens.shape, bf), pltpu.VMEM(w_qkv.shape, bf), pltpu.VMEM(w_out.shape, bf),
+            dma((7,)),
             pltpu.VMEM((2 * rows, feats), bf), pltpu.VMEM((2 * rows, feats), bf),
             pltpu.VMEM((rows, feats), bf), pltpu.VMEM((rows, feats), bf),
             pltpu.VMEM((rows, feats), bf),
@@ -444,8 +466,8 @@
             dma((blocks,)), dma((blocks,)),
         ],
         compiler_params=pltpu.CompilerParams(
-            collective_id=0, has_side_effects=True, vmem_limit_bytes=48 * 1024 * 1024),
-    )(random_blocks, global_ids, tokens, w_qkv, w_out)
+            collective_id=0, has_side_effects=True, vmem_limit_bytes=63 * 1024 * 1024 + 512 * 1024),
+    )(random_blocks.T, global_ids, tokens, w_qkv, w_out)
 
 
 def solution(mesh):

time: 64.4 us -> 59.9 us (0.930)
  local copies, waits for them, and re-layouts: 5.88 us -> 1.87 us
    unnamed x10 -> x1, local copies, waits for them, and re-layouts: 5.88 us -> 1.87 us
where the time goes in v3:
time: 59.9 us; the launch traced here: 59.7 us
  Pallas kernels  57.8 us (96%)
  local copies, waits for them, and re-layouts  1.87 us (3%)
    pallas_call x1, Pallas kernels, routed(): pl.pallas_call(route_kernel, out_shape=jax.ShapeDtypeStruct((rows, width...  57.8 us
    unnamed x1, local copies, waits for them, and re-layouts  1.87 us

profile of v3, /device:TPU:3, one launch (start us, length us, event | category | flops | bytes accessed | tf_op | source)
XLA Modules:
  0.0 59.7 jit_solution(9610166138334577989)
XLA Ops:
  0.0 57.8 %shard_map.55 = bf16[512,512]{1,0:T(8,128)(2,1)} custom-call(s32[3,8]{1,0:T(4,128)} %bitcast.1, s32[16]{0:T(128)} %gid_hbm.1, bf16[512,1024]{1,0:T(8,128)(2,1)} %tok_hbm.1, bf16[3,1024,256]{2,1,0:T(8,128)(2,1)} %wqkv_hbm.1, bf16[256,1024]{1,0:T(8,128)(2,1)} %wout_hbm.1), custom_call_target="tpu_custom_call" | custom-call | tf_op jit(solution)/shard_map/pallas_call | solution.py:447
  57.8 1.9 %copy.7 = bf16[512,512]{1,0:T(8,128)(2,1)} copy(bf16[512,512]{1,0:T(8,128)(2,1)} %shard_map.55) | data formatting | bytes 1048576

commit v4 on v3

--- a/solution.py
+++ b/solution.py
@@ -162,7 +162,7 @@
 
 def route_kernel(rand_hbm, gid_hbm, tok_hbm, wqkv_hbm, wout_hbm, out_ref,
                  rand_ref, gid_ref, tok_ref, wqkv_ref, wout_ref, ls,
-                 krow, vrow, kz, vz, q_ref, gk, gv, near_k, near_v, far_k, far_v,
+                 probs, krow, vrow, kz, vz, q_ref, gk, gv, near_k, near_v, far_k, far_v,
                  nsend_k, nsend_v, fsend_k, fsend_v, wfull, att,
                  xs, xr, zs, zr, ns, nr, fs, fr, gs, gr, ws, wr, hs, hr):
     load_tok = pltpu.make_async_copy(tok_hbm, tok_ref, ls.at[0])
@@ -247,24 +247,27 @@
     gbuf = (gk, gv)
 
     def near_copy(kind, j, crossing):
-        part = pl.ds(j * BLOCK, BLOCK)
+        part = pl.ds(aligned(j * BLOCK), BLOCK)
         n = kind * mine + j
         dst, sem = (far, fr) if crossing else (near, nr)
         return remote(nsend[kind].at[part], dst[kind].at[part], ns.at[n], sem.at[n],
                       {"seq": fwd_dev})
 
     def far_copy(kind, j):
-        part = pl.ds(j * BLOCK, BLOCK)
+        part = pl.ds(aligned(j * BLOCK), BLOCK)
         n = kind * mine + j
         return remote(fsend[kind].at[part], far[kind].at[part], fs.at[n], fr.at[n],
                       {"seq": back_dev})
 
+    def aligned(start):
+        return start if isinstance(start, int) else pl.multiple_of(start, BLOCK)
+
     def owner(j):
         gid = gid_ref[x * mine + j]
         return lax.div(gid, pair), lax.rem(gid, pair)
 
     def step_near(kind, j):
-        part = pl.ds(j * BLOCK, BLOCK)
+        part = pl.ds(aligned(j * BLOCK), BLOCK)
         line, within = owner(j)
         own = row[kind][pl.ds(within * BLOCK, BLOCK), :]
 
@@ -280,14 +283,14 @@
             near_copy(kind, j, False).start()
 
     def g_copy(kind, j):
-        spot = pl.ds(pl.multiple_of((x * mine + j) * BLOCK, BLOCK), BLOCK)
+        spot = pl.ds(aligned((x * mine + j) * BLOCK), BLOCK)
         n = kind * mine + j
         return remote(gbuf[kind].at[spot], gbuf[kind].at[spot], gs.at[n], gr.at[n],
                       {"seq": partner})
 
     def step_far(kind, j):
-        part = pl.ds(j * BLOCK, BLOCK)
-        spot = pl.ds(pl.multiple_of((x * mine + j) * BLOCK, BLOCK), BLOCK)
+        part = pl.ds(aligned(j * BLOCK), BLOCK)
+        spot = pl.ds(aligned((x * mine + j) * BLOCK), BLOCK)
         line, within = owner(j)
         own = row[kind][pl.ds(within * BLOCK, BLOCK), :]
         far_copy(kind, j).wait_recv()
@@ -325,29 +328,27 @@
         got_x[1].wait_recv()
         for j in range(mine):
             step_near(1, j)
-        send_z[1].start()
-        for kind in range(2):
-            for j in range(mine):
-                step_far(kind, j)
+        for j in range(mine):
+            step_far(0, j)
 
     @pl.when(inner)
     def _():
+        for j in range(mine):
+            step_far(0, j)
         got_x[1].wait_recv()
-        send_z[1].start()
         for j in range(mine):
             step_near(1, j)
-            step_far(0, j)
-        for j in range(mine):
-            step_far(1, j)
-
-    for kind in range(2):
+
+    def swapped(kind):
         for j in range(mine):
             n = kind * mine + j
             spot = pl.ds(pl.multiple_of(((1 - x) * mine + j) * BLOCK, BLOCK), BLOCK)
             remote(gbuf[kind].at[spot], gbuf[kind].at[spot], gs.at[n], gr.at[n],
                    {"seq": partner}).wait_recv()
-    for kind in range(2):
-        send_z[kind].wait_recv()
+
+    send_z[1].start()
+    swapped(0)
+    send_z[0].wait_recv()
 
     lane_head = lax.broadcasted_iota(jnp.int32, (BLOCK, feats), 1) // HEAD_DIM
     masks = [(lane_head == h).astype(jnp.float32) for h in range(heads)]
@@ -368,15 +369,20 @@
         return remote(att.at[core, spot], att.at[core, spot], hs.at[b], hr.at[b],
                       {"head": 1 - core})
 
-    def one_block(b, carry):
+    near_keys = (3 + RAND) * BLOCK
+    stack = heads * BLOCK
+
+    def picks(b):
+        mid = me * blocks + b
+        return [lax.rem(mid + doc_blocks - 1, doc_blocks), mid,
+                lax.rem(mid + 1, doc_blocks)] + [rand_ref[i, b] for i in range(RAND)]
+
+    def weigh(b, carry):
         spot = pl.ds(pl.multiple_of(b * BLOCK, BLOCK), BLOCK)
+        band = pl.ds(pl.multiple_of(b * stack, stack), stack)
         q = q_ref[spot, :]
         stacked = jnp.concatenate([q * m for m in masks16], axis=0)
-        mid = me * blocks + b
-        picks = [lax.rem(mid + doc_blocks - 1, doc_blocks), mid,
-                 lax.rem(mid + 1, doc_blocks)] + [rand_ref[i, b] for i in range(RAND)]
-        kloc = jnp.concatenate([fetch((krow, kz), e) for e in picks], axis=0)
-        vloc = jnp.concatenate([fetch((vrow, vz), e) for e in picks], axis=0)
+        kloc = jnp.concatenate([fetch((krow, kz), e) for e in picks(b)], axis=0)
         dims = (((1,), (1,)), ((), ()))
         sl = lax.dot_general(stacked, kloc, dims, preferred_element_type=jnp.float32)
         sg = lax.dot_general(stacked, gk[...], dims, preferred_element_type=jnp.float32)
@@ -384,9 +390,22 @@
         el = jnp.exp2((sl - top) * factor)
         eg = jnp.exp2((sg - top) * factor)
         norm = jnp.sum(el, axis=1, keepdims=True) + jnp.sum(eg, axis=1, keepdims=True)
-        o = jnp.dot(el.astype(jnp.bfloat16), vloc, preferred_element_type=jnp.float32)
-        o += jnp.dot(eg.astype(jnp.bfloat16), gv[...], preferred_element_type=jnp.float32)
-        o = o / norm
+        scale = 1.0 / norm
+        probs[band, 0:near_keys] = (el * scale).astype(jnp.bfloat16)
+        probs[band, near_keys:] = (eg * scale).astype(jnp.bfloat16)
+        step_far(1, b)
+        return carry
+
+    lax.fori_loop(0, blocks, weigh, 0)
+    swapped(1)
+    send_z[1].wait_recv()
+
+    def blend(b, carry):
+        spot = pl.ds(pl.multiple_of(b * BLOCK, BLOCK), BLOCK)
+        band = pl.ds(pl.multiple_of(b * stack, stack), stack)
+        vloc = jnp.concatenate([fetch((vrow, vz), e) for e in picks(b)], axis=0)
+        o = jnp.dot(probs[band, 0:near_keys], vloc, preferred_element_type=jnp.float32)
+        o += jnp.dot(probs[band, near_keys:], gv[...], preferred_element_type=jnp.float32)
         merged = o[0:BLOCK] * masks[0]
         for h in range(1, heads):
             merged += o[h * BLOCK:(h + 1) * BLOCK] * masks[h]
@@ -394,7 +413,7 @@
         att_copy(b).start()
         return carry
 
-    lax.fori_loop(0, blocks, one_block, 0)
+    lax.fori_loop(0, blocks, blend, 0)
 
     remote(wout_ref.at[:, pl.ds(0, half_out)], wfull.at[wother], ws.at[0], wr.at[0],
            {"head": 1 - core}).wait_recv()
@@ -453,6 +472,7 @@
             pltpu.SMEM(random_blocks.shape[::-1], jnp.int32), pltpu.SMEM(global_ids.shape, jnp.int32),
             pltpu.VMEM(tokens.shape, bf), pltpu.VMEM(w_qkv.shape, bf), pltpu.VMEM(w_out.shape, bf),
             dma((7,)),
+            pltpu.VMEM((rows * (feats // HEAD_DIM), (3 + RAND + slots) * BLOCK), bf),
             pltpu.VMEM((2 * rows, feats), bf), pltpu.VMEM((2 * rows, feats), bf),
             pltpu.VMEM((rows, feats), bf), pltpu.VMEM((rows, feats), bf),
             pltpu.VMEM((rows, feats), bf),
@@ -470,10 +490,16 @@
     )(random_blocks.T, global_ids, tokens, w_qkv, w_out)
 
 
+def layer(tokens, w_qkv, w_out, random_blocks, global_ids):
+    small = (lax.axis_size("seq") == 8 and lax.axis_size("head") == 2
+             and global_ids.shape[0] * BLOCK == 2 * tokens.shape[0])
+    run = routed if small else on_device
+    return run(tokens, w_qkv, w_out, random_blocks, global_ids)
+
+
 def solution(mesh):
-    small = mesh.shape["seq"] == 8 and mesh.shape["head"] == 2
     return jax.shard_map(
-        routed if small else on_device,
+        layer,
         mesh=mesh,
         in_specs=(
             P(("groups", "seq"), None),

time: 59.9 us -> 54.6 us (0.912)
  the two profiles are of different devices: /device:TPU:3 before, /device:TPU:1 now
where the time goes in v4:
time: 54.6 us; the launch traced here: 54.4 us
  Pallas kernels  52.6 us (96%)
  local copies, waits for them, and re-layouts  1.87 us (3%)
    pallas_call x1, Pallas kernels, routed(): pl.pallas_call(route_kernel, out_shape=jax.ShapeDtypeStruct((rows, width...  52.6 us
    unnamed x1, local copies, waits for them, and re-layouts  1.87 us

profile of v4, /device:TPU:1, one launch (start us, length us, event | category | flops | bytes accessed | tf_op | source)
XLA Modules:
  0.0 54.4 jit_solution(3551428016128215938)
XLA Ops:
  0.0 52.6 %shard_map.55 = bf16[512,512]{1,0:T(8,128)(2,1)} custom-call(s32[3,8]{1,0:T(4,128)} %bitcast.1, s32[16]{0:T(128)} %gid_hbm.1, bf16[512,1024]{1,0:T(8,128)(2,1)} %tok_hbm.1, bf16[3,1024,256]{2,1,0:T(8,128)(2,1)} %wqkv_hbm.1, bf16[256,1024]{1,0:T(8,128)(2,1)} %wout_hbm.1), custom_call_target="tpu_custom_call" | custom-call | tf_op jit(solution)/shard_map/pallas_call | solution.py:466
  52.6 1.9 %copy.7 = bf16[512,512]{1,0:T(8,128)(2,1)} copy(bf16[512,512]{1,0:T(8,128)(2,1)} %shard_map.55) | data formatting | bytes 1048576
